TPU v7x, 512 devices: a whole 4x4x16 slice. The times are simulated.
512 devices in a mesh: blk: 128 (over y, x_lo, z), quad: 4 (over x_hi, core).
Axes of the slice: x: 4 (x_hi: 2, x_lo: 2; x = x_hi * 2 + x_lo), y: 4, z: 16, core: 2. Of those that a mesh axis runs over, the one named last changes fastest.
Arguments:
- positions: float32 [3, 16384], P(None, ('blk', 'quad')), may hold values from 0 to 1
- forces: float32 [3, 16, 16384], P(None, None, ('blk', 'quad')), may hold values from -6 to 6
Outputs:
- velocity: float32 [3, 16, 16384], P(None, None, ('blk', 'quad'))
All inputs are finite; a program needn't handle non-finite values.
Results may differ from a plain program's by a relative error of at most 0.0003.
Values sent between devices are 32-bit elements; how exact they have to be, the bound alone decides.
A program may use at most 64 MiB of HBM per device.

v0:
```python
import math
import jax
import jax.numpy as jnp
from jax import lax
from jax.sharding import PartitionSpec as P

radius_scale = 0.3


def laid_out(tiles, dim):
    lengths = list(tiles.shape[1:])
    lengths[dim] *= tiles.shape[0]
    return jnp.moveaxis(tiles, 0, dim).reshape(lengths)


def copy_for_each(value, axis):
    peers = lax.axis_size(axis)
    return lax.all_to_all(
        jnp.broadcast_to(value[None], (peers, *value.shape)), axis, 0, 0, tiled=True
    )


def gather_directly(value, axis, dim):
    return laid_out(copy_for_each(value, axis), dim)


def gather_turned(arrays, axis, dims):
    turned = [jnp.moveaxis(a, dim, 0) for a, dim in zip(arrays, dims)]
    widths = [t[0].size for t in turned]
    both = jnp.concatenate([t.reshape(-1, w) for t, w in zip(turned, widths)], axis=1)
    whole = lax.all_gather(both, axis, axis=0, tiled=True)
    tiles = jnp.split(whole, [sum(widths[:k]) for k in range(1, len(widths))], axis=1)
    return tuple(
        (
            jnp.moveaxis(b.reshape(-1, *t.shape[1:]), 0, dim)
            for b, t, dim in zip(tiles, turned, dims)
        )
    )


def in_blocks(value, dim, peers):
    before, after = (value.shape[:dim], value.shape[dim + 1 :])
    return jnp.moveaxis(value.reshape(*before, peers, -1, *after), dim, 0)


def sent_and_summed(value, axis, dim):
    peers = lax.axis_size(axis)
    tiles = lax.all_to_all(in_blocks(value, dim, peers), axis, 0, 0, tiled=True)
    return jnp.sum(tiles, axis=0)


def mobility_tile(home_pos, visit_pos, radius):
    separation = home_pos[:, :, None] - visit_pos[:, None, :]
    squared = jnp.sum(separation * separation, axis=0)
    distance = jnp.sqrt(squared)
    far_dist = jnp.maximum(distance, 2.0 * radius)
    inverse = 1.0 / far_dist
    ratio_sq = radius * radius * inverse * inverse
    factor = 0.75 * radius * inverse
    iso_far = factor * (1.0 + 2.0 / 3.0 * ratio_sq)
    dyad_far = factor * (1.0 - 2.0 * ratio_sq) * inverse * inverse
    iso_near = 1.0 - 9.0 / 32.0 * distance / radius
    dyad_near = 3.0 / 32.0 / (radius * jnp.maximum(distance, radius / 1000.0))
    near_mask = distance < 2.0 * radius
    coef_iso = jnp.where(near_mask, iso_near, iso_far)
    coef_dyad = jnp.where(near_mask, dyad_near, dyad_far)
    identity = jnp.eye(3, dtype=jnp.float32)
    return (
        coef_dyad[None, None] * separation[:, None] * separation[None, :]
        + identity[:, :, None, None] * coef_iso[None, None]
    )


def body(positions, forces):
    vectors = forces.shape[1]
    local_rows = positions.shape[1]
    total = local_rows * lax.axis_size("blk") * lax.axis_size("quad")
    radius = radius_scale / total ** (1.0 / 3.0)
    flat_force = forces.reshape(3 * vectors, local_rows)
    block_pos = gather_directly(positions, "quad", 1)
    block_rows = block_pos.shape[1]
    partial_sum = jnp.zeros((3, vectors, block_rows), jnp.float32)
    part_pos, part_force = gather_turned((positions, flat_force), "blk", (1, 1))
    count = part_pos.shape[1]
    width = math.gcd(count, 512)

    def one_block(index, running):
        col_pos = lax.dynamic_slice_in_dim(part_pos, index * width, width, 1)
        col_force = lax.dynamic_slice_in_dim(part_force, index * width, width, 1).reshape(
            3, vectors, width
        )
        kernel = mobility_tile(block_pos, col_pos, radius)
        return running + jnp.einsum(
            "cdij,dvj->cvi", kernel, col_force, precision=lax.Precision.HIGHEST
        )

    partial_sum = lax.fori_loop(0, count // width, one_block, partial_sum)
    velocity = sent_and_summed(partial_sum, "quad", 2)
    return velocity


def solution(mesh):
    in_specs = (P(None, ("blk", "quad")), P(None, None, ("blk", "quad")))
    out_specs = P(None, None, ("blk", "quad"))
    return jax.shard_map(body, mesh=mesh, in_specs=in_specs, out_specs=out_specs, check_vma=False)
```

profile of v0, /device:TPU:1, one launch (start us, length us, event | category | flops | bytes accessed | tf_op | source)
XLA Modules:
  0.0 370.5 jit_solution(10042499356964226688)
XLA Ops:
  0.0 1.3 broadcast_in_dim.28
  1.3 10.1 %all-to-all-start = ((f32[4,3,32]{2,1,0:T(4,128)}), f32[4,3,32]{2,1,0:T(4,128)S(1)}, u32[]{:S(2)}, u32[]{:S(2)}) async-start(f32[4,3,32]{2,1,0:T(4,128)} %broadcast_in_dim.28), calls=%async_computation | async-start | bytes 16384 | tf_op jit(solution)/shard_map/all_to_all | solution.py:18
  11.4 0.7 pad_maximum_fusion
  12.2 262.2 %all_gather.3 = f32[4096,51]{1,0:T(8,128)S(1)} all-gather(f32[32,51]{1,0:T(8,128)S(1)} %copy.8), channel_id=1, replica_groups=mesh['blk'=128,'quad'=4] {'blk'}, dimensions={0}, use_global_device_ids=true | all-gather | bytes 842112 | tf_op jit(solution)/shard_map/all_gather | solution.py:31
  274.4 1.5 slice_bitcast_fusion
  275.9 0.6 slice_bitcast_fusion.1
  276.5 2.2 copy.11
  278.7 0.6 copy.9
  279.5 0.5 copy-done
  280.0 22.7 %while.17 = (s32[]{:T(128)}, f32[3,16,128]{2,1,0:T(8,128)S(1)}, f32[48,4096]{1,0:T(8,128)S(1)}, f32[3,4,32]{2,1,0:T(4,128)}, f32[3,4096]{1,0:T(4,128)S(1)}, /*in...) while((s32[]{:T(128)}, f32[3,16,128]{2,1,0:T(8,128)S(1)}, ...), condition=%wide.wide.region_2.3_spmd.clone, body=%wide.wide.region_0.2_spmd.clone.sunk | while | flops 117321752 | bytes 5090549 | solution.py:97
  280.1 0.3 fusion.29
  280.4 0.2 subtract_multiply_fusion.3
  280.6 2.2 fusion.31
  283.0 0.3 fusion.29
  283.2 0.2 subtract_multiply_fusion.3
  283.4 2.2 fusion.31
  285.8 0.3 fusion.29
  286.3 2.2 fusion.31
  288.7 0.3 fusion.29
  289.1 2.2 fusion.31
  291.5 0.3 fusion.29
  291.9 2.2 fusion.31
  294.4 0.3 fusion.29
  294.8 2.2 fusion.31
  297.2 0.3 fusion.29
  297.6 2.2 fusion.31
  300.0 0.3 fusion.29
  300.5 2.2 fusion.31
  302.9 65.6 %all_to_all.10 = f32[4,1,1536]{2,1,0:T(1,128)S(1)} all-to-all(f32[4,1,1536]{2,1,0:T(1,128)S(1)} %reshape.73), channel_id=1, replica_groups=mesh['blk'=128,'quad'=4] {'quad'}, dimensions={0} | all-to-all | bytes 49152 | tf_op jit(solution)/shard_map/all_to_all | solution.py:48
  368.5 0.5 broadcast.294
  369.0 0.7 reduce
  369.8 0.6 reduce_sum.25
  (48 shorter events, 2.9 us)
Async XLA Ops:
  1.3 278.1 %all-to-all-start = ((f32[4,3,32]{2,1,0:T(4,128)}), f32[4,3,32]{2,1,0:T(4,128)S(1)}, u32[]{:S(2)}, u32[]{:S(2)}) async-start(f32[4,3,32]{2,1,0:T(4,128)} %broadcast_in_dim.28), calls=%async_computation | async-start | bytes 16384 | tf_op jit(solution)/shard_map/all_to_all | solution.py:18
  279.4 0.6 copy-start
where the time goes:
time: 371 us; the launch traced here: 370 us
  blocking collectives  328 us (88%)
  matrix products  17.5 us (5%)
  starting transfers between devices  10.1 us (3%)
  local copies, waits for them, and re-layouts  7.87 us (2%)
  other arithmetic  6.63 us (2%)
    all_gather x1, blocking collectives, gather_turned(): whole = lax.all_gather(both, axis, axis=0, tiled=True)  262 us
    all_to_all x1, blocking collectives, sent_and_summed(): tiles = lax.all_to_all(in_blocks(value, dim, peers), axis, 0, 0, tiled=True)  65.6 us
    dot_general x8, matrix products, one_block(): jnp.einsum('cdij,dvj->cvi', kernel, col_force, precision=lax.Precision.HI...  17.5 us
    all_to_all x1, starting transfers between devices, copy_for_each(): lax.all_to_all(jnp.broadcast_to(value[None], (peers, *value.shape)), axis...  10.1 us
  transfers between devices with their start and end apart: 1, of which 0 were waited for; matrix products, arithmetic and copies ran while one was open for 2% of the time, Pallas kernels for 0%

commit v1 on v0

--- a/solution.py
+++ b/solution.py
@@ -28,7 +28,9 @@
     turned = [jnp.moveaxis(a, dim, 0) for a, dim in zip(arrays, dims)]
     widths = [t[0].size for t in turned]
     both = jnp.concatenate([t.reshape(-1, w) for t, w in zip(turned, widths)], axis=1)
-    whole = lax.all_gather(both, axis, axis=0, tiled=True)
+    whole = jnp.concatenate(
+        lax.all_to_all(jnp.stack([both] * lax.axis_size(axis)), axis, 0, 0), axis=0
+    )
     tiles = jnp.split(whole, [sum(widths[:k]) for k in range(1, len(widths))], axis=1)
     return tuple(
         (

time: 371 us -> 126 us (0.34)
  blocking collectives: 328 us -> 12.8 us
  waiting for transfers between devices: 0.01 us -> 42 us
  starting transfers between devices: 10.1 us -> 25.7 us
  local copies, waits for them, and re-layouts: 7.87 us -> 16.2 us
    all_gather x1 -> x0, blocking collectives: 262 us -> none  [gather_turned(): whole = lax.all_gather(both, axis, axis=0, tiled=True)]
    all_to_all x1, blocking collectives: 65.6 us -> 12.8 us  [sent_and_summed(): tiles = lax.all_to_all(in_blocks(value, dim, peers), axis, 0, 0, tiled=True)]
    all_to_all x0 -> x1, waiting for transfers between devices: none -> 42 us  [gather_turned(): lax.all_to_all(jnp.stack([both] * lax.axis_size(axis)), axis, 0, 0)]
    all_to_all x0 -> x1, starting transfers between devices: none -> 15.6 us  [gather_turned(): lax.all_to_all(jnp.stack([both] * lax.axis_size(axis)), axis, 0, 0)]
    unnamed x7 -> x11, local copies, waits for them, and re-layouts: 3.5 us -> 10.2 us
  transfers between devices with their start and end apart: 1 -> 2, of which waited for: 0 -> 1; matrix products, arithmetic and copies ran while one was open for 2% -> 4% of each run, Pallas kernels for 0% -> 0%
where the time goes in v1:
time: 126 us; the launch traced here: 124 us
  waiting for transfers between devices  42 us (33%)
  starting transfers between devices  25.7 us (20%)
  matrix products  17.5 us (14%)
  local copies, waits for them, and re-layouts  16.2 us (13%)
  blocking collectives  12.8 us (10%)
  other arithmetic  9.24 us (7%)
    all_to_all x1, waiting for transfers between devices, gather_turned(): lax.all_to_all(jnp.stack([both] * lax.axis_size(axis)), axis, 0, 0)  42 us
    dot_general x8, matrix products, one_block(): jnp.einsum('cdij,dvj->cvi', kernel, col_force, precision=lax.Precision.HI...  17.5 us
    all_to_all x1, starting transfers between devices, gather_turned(): lax.all_to_all(jnp.stack([both] * lax.axis_size(axis)), axis, 0, 0)  15.6 us
    all_to_all x1, blocking collectives, sent_and_summed(): tiles = lax.all_to_all(in_blocks(value, dim, peers), axis, 0, 0, tiled=True)  12.8 us
    unnamed x11, local copies, waits for them, and re-layouts  10.2 us
    all_to_all x1, starting transfers between devices, copy_for_each(): lax.all_to_all(jnp.broadcast_to(value[None], (peers, *value.shape)), axis...  10.1 us
    transpose x2, local copies, waits for them, and re-layouts, gather_turned(): jnp.moveaxis(b.reshape(-1, *t.shape[1:]), 0, dim)  3.39 us
    all_to_all x1, other arithmetic, gather_turned(): lax.all_to_all(jnp.stack([both] * lax.axis_size(axis)), axis, 0, 0)  2.64 us
  transfers between devices with their start and end apart: 2, of which 1 were waited for; matrix products, arithmetic and copies ran while one was open for 4% of the time, Pallas kernels for 0%

profile of v1, /device:TPU:1, one launch (start us, length us, event | category | flops | bytes accessed | tf_op | source)
XLA Modules:
  0.0 124.0 jit_solution(762381580804943291)
XLA Ops:
  0.0 1.3 %broadcast_in_dim.28 = f32[4,3,32]{2,1,0:T(4,128)} broadcast(f32[3,32]{1,0:T(4,128)} %param.4), dimensions={1,2} | broadcast | bytes 1920 | tf_op jit(solution)/shard_map/broadcast_in_dim | solution.py:19
  1.3 10.1 %all-to-all-start.1 = ((f32[4,3,32]{2,1,0:T(4,128)}), f32[4,3,32]{2,1,0:T(4,128)S(1)}, u32[]{:S(2)}, u32[]{:S(2)}) async-start(f32[4,3,32]{2,1,0:T(4,128)} %broadcast_in_dim.28), calls=%async_computation.1 | async-start | bytes 16384 | tf_op jit(solution)/shard_map/all_to_all | solution.py:18
  11.4 0.7 pad_maximum_fusion
  12.5 4.1 %reshape.79 = f32[128,1,1632]{2,1,0:T(1,128)} reshape(f32[128,32,51]{2,1,0:T(8,128)S(1)} %stack.2) | data formatting | bytes 1671168
  16.5 15.6 %all-to-all-start = ((f32[128,1,1632]{2,1,0:T(1,128)}), f32[128,1,1632]{2,1,0:T(1,128)S(1)}, u32[]{:S(2)}, u32[]{:S(2)}) async-start(f32[128,1,1632]{2,1,0:T(1,128)} %reshape.79), calls=%async_computation | async-start | bytes 1703936 | tf_op jit(solution)/shard_map/all_to_all | solution.py:32
  32.3 42.0 %all-to-all-done = f32[128,1,1632]{2,1,0:T(1,128)S(1)} async-done(((f32[128,1,1632]{2,1,0:T(1,128)}), f32[128,1,1632]{2,1,0:T(1,128)S(1)}, u32[]{:S(2)}, u32[]{:S(2)}) %all-to-all-start) | async-done | bytes 835616 | tf_op jit(solution)/shard_map/all_to_all | solution.py:32
  74.3 0.5 broadcast.296
  74.8 2.6 %reduce = f32[128,1632]{1,0:T(8,128)S(1)} reduce(f32[128,1,1632]{2,1,0:T(1,128)S(1)} %all-to-all-done, f32[]{:T(128)} %broadcast.296), dimensions={1}, to_apply=%all_to_all.9.reduce_sub_computation | reduce | bytes 1671172 | tf_op jit(solution)/shard_map/all_to_all | solution.py:32
  77.4 3.0 %reshape.80 = f32[128,32,51]{2,1,0:T(8,128)S(1)} reshape(f32[128,1632]{1,0:T(8,128)S(1)} %reduce) | data formatting | bytes 1671168
  80.4 1.4 %slice_bitcast_fusion = f32[3,4096]{0,1:T(8,128)} fusion(f32[4096,51]{1,0:T(8,128)S(1)} %bitcast.31), kind=kLoop, calls=%fused_computation.23 | loop fusion | bytes 98304 | tf_op jit(solution)/shard_map/transpose | solution.py:37
  81.8 2.0 %slice_bitcast_fusion.1 = f32[48,4096]{0,1:T(8,128)} fusion(f32[4096,51]{1,0:T(8,128)S(1)} %bitcast.32), kind=kLoop, calls=%fused_computation.24 | loop fusion | bytes 1572864 | tf_op jit(solution)/shard_map/transpose | solution.py:37
  83.8 2.4 %copy.13 = f32[3,4096]{1,0:T(4,128)S(1)} copy(f32[3,4096]{0,1:T(8,128)} %slice_bitcast_fusion) | data formatting | bytes 98304
  86.2 0.6 copy.11
  86.8 22.8 %while.17 = (s32[]{:T(128)}, f32[3,16,128]{2,1,0:T(8,128)S(1)}, f32[48,4096]{1,0:T(8,128)S(1)}, f32[3,4,32]{2,1,0:T(4,128)}, f32[3,4096]{1,0:T(4,128)S(1)}, /*in...) while((s32[]{:T(128)}, f32[3,16,128]{2,1,0:T(8,128)S(1)}, ...), condition=%wide.wide.region_2.3_spmd.clone, body=%wide.wide.region_0.2_spmd.clone.sunk | while | flops 117321752 | bytes 5090549 | solution.py:99
  87.0 0.3 fusion.29
  87.4 2.2 %fusion.31 = f32[3,16,128]{2,1,0:T(8,128)S(1)} fusion(f32[3,16,512,1]{2,1,0,3:T(8,128)S(1)} %bitcast.33, f32[128,512]{1,0:T(8,128)S(1)} %get-tuple-element.250, f32[3,3]{1,0:T(4,128)S(1)} %fusion.30, f32[3,128,512]{2,1,0:T(8,128)S(1)} %get-tuple-element.252, f32[3,128,512]{2,1,0:T(8,128)S(1)} %get-tuple-element.253, ...), kind=kOutput, calls=%fused_computation.9.clone.clone.1 | convolution fusion | flops 115027968 | bytes 1982501 | tf_op jit(solution)/shard_map/while/body/eval_jaxpr/cdij,dvj->cvi/dot_general | solution.py:95
  89.8 0.3 fusion.29
  90.3 2.2 %fusion.31 = f32[3,16,128]{2,1,0:T(8,128)S(1)} fusion(f32[3,16,512,1]{2,1,0,3:T(8,128)S(1)} %bitcast.33, f32[128,512]{1,0:T(8,128)S(1)} %get-tuple-element.250, f32[3,3]{1,0:T(4,128)S(1)} %fusion.30, f32[3,128,512]{2,1,0:T(8,128)S(1)} %get-tuple-element.252, f32[3,128,512]{2,1,0:T(8,128)S(1)} %get-tuple-element.253, ...), kind=kOutput, calls=%fused_computation.9.clone.clone.1 | convolution fusion | flops 115027968 | bytes 1982501 | tf_op jit(solution)/shard_map/while/body/eval_jaxpr/cdij,dvj->cvi/dot_general | solution.py:95
  92.7 0.3 fusion.29
  93.1 2.2 %fusion.31 = f32[3,16,128]{2,1,0:T(8,128)S(1)} fusion(f32[3,16,512,1]{2,1,0,3:T(8,128)S(1)} %bitcast.33, f32[128,512]{1,0:T(8,128)S(1)} %get-tuple-element.250, f32[3,3]{1,0:T(4,128)S(1)} %fusion.30, f32[3,128,512]{2,1,0:T(8,128)S(1)} %get-tuple-element.252, f32[3,128,512]{2,1,0:T(8,128)S(1)} %get-tuple-element.253, ...), kind=kOutput, calls=%fused_computation.9.clone.clone.1 | convolution fusion | flops 115027968 | bytes 1982501 | tf_op jit(solution)/shard_map/while/body/eval_jaxpr/cdij,dvj->cvi/dot_general | solution.py:95
  95.5 0.3 fusion.29
  96.0 2.2 %fusion.31 = f32[3,16,128]{2,1,0:T(8,128)S(1)} fusion(f32[3,16,512,1]{2,1,0,3:T(8,128)S(1)} %bitcast.33, f32[128,512]{1,0:T(8,128)S(1)} %get-tuple-element.250, f32[3,3]{1,0:T(4,128)S(1)} %fusion.30, f32[3,128,512]{2,1,0:T(8,128)S(1)} %get-tuple-element.252, f32[3,128,512]{2,1,0:T(8,128)S(1)} %get-tuple-element.253, ...), kind=kOutput, calls=%fused_computation.9.clone.clone.1 | convolution fusion | flops 115027968 | bytes 1982501 | tf_op jit(solution)/shard_map/while/body/eval_jaxpr/cdij,dvj->cvi/dot_general | solution.py:95
  98.4 0.3 fusion.29
  98.8 2.2 %fusion.31 = f32[3,16,128]{2,1,0:T(8,128)S(1)} fusion(f32[3,16,512,1]{2,1,0,3:T(8,128)S(1)} %bitcast.33, f32[128,512]{1,0:T(8,128)S(1)} %get-tuple-element.250, f32[3,3]{1,0:T(4,128)S(1)} %fusion.30, f32[3,128,512]{2,1,0:T(8,128)S(1)} %get-tuple-element.252, f32[3,128,512]{2,1,0:T(8,128)S(1)} %get-tuple-element.253, ...), kind=kOutput, calls=%fused_computation.9.clone.clone.1 | convolution fusion | flops 115027968 | bytes 1982501 | tf_op jit(solution)/shard_map/while/body/eval_jaxpr/cdij,dvj->cvi/dot_general | solution.py:95
  101.2 0.3 fusion.29
  101.7 2.2 %fusion.31 = f32[3,16,128]{2,1,0:T(8,128)S(1)} fusion(f32[3,16,512,1]{2,1,0,3:T(8,128)S(1)} %bitcast.33, f32[128,512]{1,0:T(8,128)S(1)} %get-tuple-element.250, f32[3,3]{1,0:T(4,128)S(1)} %fusion.30, f32[3,128,512]{2,1,0:T(8,128)S(1)} %get-tuple-element.252, f32[3,128,512]{2,1,0:T(8,128)S(1)} %get-tuple-element.253, ...), kind=kOutput, calls=%fused_computation.9.clone.clone.1 | convolution fusion | flops 115027968 | bytes 1982501 | tf_op jit(solution)/shard_map/while/body/eval_jaxpr/cdij,dvj->cvi/dot_general | solution.py:95
  104.5 2.2 %fusion.31 = f32[3,16,128]{2,1,0:T(8,128)S(1)} fusion(f32[3,16,512,1]{2,1,0,3:T(8,128)S(1)} %bitcast.33, f32[128,512]{1,0:T(8,128)S(1)} %get-tuple-element.250, f32[3,3]{1,0:T(4,128)S(1)} %fusion.30, f32[3,128,512]{2,1,0:T(8,128)S(1)} %get-tuple-element.252, f32[3,128,512]{2,1,0:T(8,128)S(1)} %get-tuple-element.253, ...), kind=kOutput, calls=%fused_computation.9.clone.clone.1 | convolution fusion | flops 115027968 | bytes 1982501 | tf_op jit(solution)/shard_map/while/body/eval_jaxpr/cdij,dvj->cvi/dot_general | solution.py:95
  106.9 0.3 fusion.29
  107.3 2.2 %fusion.31 = f32[3,16,128]{2,1,0:T(8,128)S(1)} fusion(f32[3,16,512,1]{2,1,0,3:T(8,128)S(1)} %bitcast.33, f32[128,512]{1,0:T(8,128)S(1)} %get-tuple-element.250, f32[3,3]{1,0:T(4,128)S(1)} %fusion.30, f32[3,128,512]{2,1,0:T(8,128)S(1)} %get-tuple-element.252, f32[3,128,512]{2,1,0:T(8,128)S(1)} %get-tuple-element.253, ...), kind=kOutput, calls=%fused_computation.9.clone.clone.1 | convolution fusion | flops 115027968 | bytes 1982501 | tf_op jit(solution)/shard_map/while/body/eval_jaxpr/cdij,dvj->cvi/dot_general | solution.py:95
  109.8 12.8 %all_to_all.15 = f32[4,1,1536]{2,1,0:T(1,128)S(1)} all-to-all(f32[4,1,1536]{2,1,0:T(1,128)S(1)} %reshape.81), channel_id=1, replica_groups=mesh['blk'=128,'quad'=4] {'quad'}, dimensions={0} | all-to-all | bytes 49152 | tf_op jit(solution)/shard_map/all_to_all | solution.py:50
  122.6 0.7 reduce.1
  123.4 0.6 reduce_sum.25
  (55 shorter events, 3.7 us)
Async XLA Ops:
  1.3 15.3 %all-to-all-start.1 = ((f32[4,3,32]{2,1,0:T(4,128)}), f32[4,3,32]{2,1,0:T(4,128)S(1)}, u32[]{:S(2)}, u32[]{:S(2)}) async-start(f32[4,3,32]{2,1,0:T(4,128)} %broadcast_in_dim.28), calls=%async_computation.1 | async-start | bytes 16384 | tf_op jit(solution)/shard_map/all_to_all | solution.py:18
  16.5 57.7 %all-to-all-start = ((f32[128,1,1632]{2,1,0:T(1,128)}), f32[128,1,1632]{2,1,0:T(1,128)S(1)}, u32[]{:S(2)}, u32[]{:S(2)}) async-start(f32[128,1,1632]{2,1,0:T(1,128)} %reshape.79), calls=%async_computation | async-start | bytes 1703936 | tf_op jit(solution)/shard_map/all_to_all | solution.py:32
  32.2 48.3 %copy-start.1 = (f32[3,4,32]{2,1,0:T(4,128)}, f32[3,4,32]{2,1,0:T(4,128)S(1)}, u32[]{:S(2)}) copy-start(f32[3,4,32]{2,1,0:T(4,128)S(1)} %copy.12) | copy-start | bytes 4612
  83.8 2.4 %copy-start = (f32[48,4096]{0,1:T(8,128)S(1)}, f32[48,4096]{0,1:T(8,128)}, u32[]{:S(2)}) copy-start(f32[48,4096]{0,1:T(8,128)} %slice_bitcast_fusion.1) | copy-start | bytes 2359300
